TPU v7x, 32 devices: a whole 2x2x4 slice. The times are simulated.
32 devices in a mesh: parts: 2 (over y), seq: 4 (over z), layer: 4 (over x, core).
Axes of the slice: x: 2, y: 2, z: 4, core: 2. Of those that a mesh axis runs over, the one named last changes fastest.
Arguments:
- store: bfloat16 [2048, 16384], P(('parts', 'seq'), 'layer'), parts along dimension 0, may hold values from -0.046875 to 0.046875
- queries: float32 [256, 16384], P('seq', 'layer'), may hold values from -6 to 6
- owner: int32 [8], replicated, may hold values from 0 to 7, each once
- eig_in: float32 [8, 32, 32], replicated, may hold values from -1 to 1
- eig_out: float32 [8, 64, 64], replicated, may hold values from -0.75 to 0.75
- eig_val: float32 [8, 32, 64], replicated, may hold values from 0.05 to 1
- query_order: int32 [256], replicated, may hold values from 0 to 255, each once
Outputs:
- scores: float32 [2048, 256], P(('parts', 'seq', 'layer')), parts along dimension 0
There are 2 independent parts, one for each index of `parts`. A program takes and returns all parts, laid end to end along the dimension named above; an argument that names none is the same for every part. Nothing has to cross between parts.
Inputs may be any that keep to these rules, and one draw needn't show every extreme that they name: `owner`: each layer appears once. `query_order`: each query appears once.
All inputs are finite; a program needn't handle non-finite values.
Results may differ from a plain program's by a relative error of at most 0.0029.
Values may be sent and summed in bfloat16 or wider, within the bound.
A program may use at most 64 MiB of HBM per device.

v0:
```python
import jax
import jax.numpy as jnp
from jax import lax
from jax.sharding import PartitionSpec as P

A = 32
B = 64


def precondition(grads, basis_in, basis_out, values):
    rotated = jnp.einsum(
        "tai,qtab,tbj->qtij", basis_in, grads, basis_out, precision=lax.Precision.HIGHEST
    )
    scaled = rotated / (values + 0.1)
    return jnp.einsum(
        "tia,qtab,tjb->qtij", basis_in, scaled, basis_out, precision=lax.Precision.HIGHEST
    )


def on_device(store, queries, owner, eig_in, eig_out, eig_val, query_order):
    width = A * B
    slots_here = store.shape[1] // width
    slot_ids = lax.axis_index("layer") * slots_here + jnp.arange(slots_here, dtype=jnp.int32)
    model_ids = jnp.take(owner, slot_ids, axis=0)
    basis_in = jnp.take(eig_in, model_ids, axis=0)
    basis_out = jnp.take(eig_out, model_ids, axis=0)
    values = jnp.take(eig_val, model_ids, axis=0)
    gathered = lax.all_gather(queries, "seq", axis=0, tiled=True)
    grads = gathered.reshape(gathered.shape[0], slots_here, A, B)
    ready = (
        precondition(grads, basis_in, basis_out, values)
        .reshape(gathered.shape[0], slots_here * width)
        .astype(jnp.bfloat16)
    )
    ordered = jnp.take(ready, query_order, axis=0)
    return lax.psum_scatter(
        lax.dot_general(
            store, ordered, (((1,), (1,)), ((), ())), preferred_element_type=jnp.float32
        ),
        "layer",
        scatter_dimension=0,
        tiled=True,
    )


def solution(mesh):
    in_specs = (P(("parts", "seq"), "layer"), P("seq", "layer"), P(), P(), P(), P(), P())
    out_specs = P(("parts", "seq", "layer"), None)
    return jax.shard_map(
        on_device, mesh=mesh, in_specs=in_specs, out_specs=out_specs, check_vma=False
    )
```

profile of v0, /device:TPU:0, one launch (start us, length us, event | category | flops | bytes accessed | tf_op | source)
XLA Modules:
  0.0 166.6 jit_solution(10413760787454562738)
XLA Ops:
  6.5 0.0 copy-start
  6.5 0.0 all-gather.2.cloned.1.call-start
  6.5 0.7 all-gather.2.cloned.1.call-update
  7.3 0.0 reduce-scatter.4.cloned.1.call-start
  7.3 1.3 gather_fusion
  8.7 1.5 gather_fusion.1
  10.1 1.5 gather_fusion.3
  11.6 1.5 gather_fusion.2
  13.1 0.7 compare_select_fusion
  13.8 0.7 compare_and_fusion.1
  14.5 0.1 select_add_fusion
  14.6 77.9 %all-gather.2.cloned.1.call-done = f32[256,4096]{1,0:T(8,128)} async-done(((f32[64,4096]{1,0:T(8,128)}), f32[256,4096]{1,0:T(8,128)}) %all-gather.2.cloned.1.call-update) | async-done | bytes 4194320 | tf_op jit(solution)/shard_map/all_gather | solution.py:28
  92.4 5.6 %copy.13 = f32[256,4096]{0,1:T(8,128)} copy(f32[256,4096]{1,0:T(8,128)} %all-gather.2.cloned.1.call-done) | data formatting | bytes 8388608 | tf_op jit(solution)/shard_map/all_gather | solution.py:28
  98.0 8.6 %fusion.8 = f32[256,2,64,32]{0,3,2,1:T(8,128)S(1)} fusion(f32[256,2,32,64]{0,3,2,1:T(8,128)} %bitcast.42, f32[2,32,32]{2,1,0:T(8,128)S(1)} %gather_fusion.1, pred[2]{0:T(512)(128)(4,1)S(1)} %compare_and_fusion), kind=kOutput, calls=%fused_computation.14 | convolution fusion | flops 402655232 | bytes 8396802 | tf_op jit(solution)/shard_map/tai,qtab,tbj->qtij/dot_general | solution.py:11
  106.6 6.8 %divide_bitcast_fusion = f32[256,2,32,64]{0,3,2,1:T(8,128)S(1)} fusion(f32[2,32,64]{2,1,0:T(8,128)S(1)} %select_add_fusion, f32[256,2,64,32]{0,3,2,1:T(8,128)S(1)} %fusion.8, f32[2,64,64]{2,1,0:T(8,128)S(1)} %gather_fusion.2, pred[2]{0:T(512)(128)(4,1)S(1)} %compare_and_fusion), kind=kOutput, calls=%fused_computation.13 | convolution fusion | flops 806363136 | bytes 8437762 | tf_op jit(solution)/shard_map/tai,qtab,tbj->qtij/dot_general | solution.py:11
  113.4 6.6 %fusion.11 = f32[256,2,64,32]{0,3,2,1:T(8,128)S(1)} fusion(f32[256,2,32,64]{0,3,2,1:T(8,128)S(1)} %divide_bitcast_fusion, f32[2,32,32]{2,1,0:T(8,128)S(1)} %gather_fusion.1, pred[2]{0:T(512)(128)(4,1)S(1)} %compare_and_fusion), kind=kOutput, calls=%fused_computation.15 | convolution fusion | flops 402655232 | bytes 8396802 | tf_op jit(solution)/shard_map/tia,qtab,tjb->qtij/dot_general | solution.py:15
  120.0 6.8 %fusion.19 = bf16[2,256,32,64]{1,3,2,0:T(8,128)(2,1)} fusion(f32[256,2,64,32]{0,3,2,1:T(8,128)S(1)} %fusion.11, f32[2,64,64]{2,1,0:T(8,128)S(1)} %gather_fusion.2, pred[2]{0:T(512)(128)(4,1)S(1)} %compare_and_fusion), kind=kOutput, calls=%fused_computation.19 | convolution fusion | flops 806363136 | bytes 6324226 | tf_op jit(solution)/shard_map/tia,qtab,tjb->qtij/dot_general | solution.py:15
  126.7 4.1 %copy.20 = bf16[256,4096]{1,0:T(8,128)(2,1)} copy(bf16[256,4096]{0,1:T(8,128)(2,1)} %bitcast.43) | data formatting | bytes 4194304 | tf_op jit(solution)/shard_map/convert_element_type | solution.py:33
  130.8 7.0 %gather_fusion.4 = bf16[256,4096]{1,0:T(8,128)(2,1)} fusion(bf16[256,4096]{1,0:T(8,128)(2,1)} %copy.20, s32[1024]{0:T(1024)S(1)} %pad_clamp_fusion), kind=kCustom, calls=%fused_computation.4 | custom fusion | bytes 4195328 | tf_op jit(solution)/shard_map/jit(_take)/gather | solution.py:35
  137.9 0.0 copy-done
  137.9 2.3 %fusion.22 = f32[256,256]{0,1:T(8,128)S(1)} fusion(bf16[256,4096]{1,0:T(8,128)(2,1)S(1)} %copy-done, bf16[256,4096]{1,0:T(8,128)(2,1)} %gather_fusion.4, pred[256]{0:T(512)(128)(4,1)S(1)} %compare_and_fusion.1), kind=kOutput, calls=%fused_computation.20 | convolution fusion | flops 537919488 | bytes 4456704 | tf_op jit(solution)/shard_map/dot_general | solution.py:37
  140.2 0.8 copy.30
  141.1 0.0 reduce-scatter.4.cloned.1.call-update
  141.1 18.7 %reduce-scatter.4.cloned.1.call-done = f32[64,256]{1,0:T(8,128)} async-done(((f32[256,256]{1,0:T(8,128)}), f32[64,256]{1,0:T(8,128)}) %reduce-scatter.4.cloned.1.call-update) | async-done | bytes 65552 | tf_op jit(solution)/shard_map/reduce_scatter | solution.py:36
  (6 shorter events, 0.1 us)
Async XLA Ops:
  6.5 131.3 %copy-start = (bf16[256,4096]{1,0:T(8,128)(2,1)S(1)}, bf16[256,4096]{1,0:T(8,128)(2,1)}, u32[]{:S(2)}) copy-start(bf16[256,4096]{1,0:T(8,128)(2,1)} %param.7) | copy-start | bytes 6291460
  6.5 85.9 %all-gather.2.cloned.1.call-start = ((), (), s32[]{:S(2)}) async-start(), calls=%async_computation.1 | async-start | bytes 5242880 | tf_op jit(solution)/shard_map/all_gather | solution.py:28
  7.3 152.5 %reduce-scatter.4.cloned.1.call-start = ((), (), s32[]{:S(2)}) async-start(), calls=%async_computation.2 | async-start | bytes 327680 | tf_op jit(solution)/shard_map/reduce_scatter | solution.py:36
Sparse Core Ops, SparseCore 0:
  8.9 83.4 all-gather.1
  141.2 18.5 reduce-scatter.3
where the time goes:
time: 167 us
  waiting for transfers between devices  97.3 us (58%)
  matrix products  31 us (19%)
  local copies, waits for them, and re-layouts  23.3 us (14%)
  between operations  13.5 us (8%)
    all_gather x1, waiting for transfers between devices, on_device(): gathered = lax.all_gather(queries, 'seq', axis=0, tiled=True)  77.9 us
    reduce_scatter x1, waiting for transfers between devices, on_device(): lax.psum_scatter(lax.dot_general(store, ordered, (((1,), (1,)), ((), ()))...  18.7 us
    dot_general x2, matrix products, precondition(): jnp.einsum('tai,qtab,tbj->qtij', basis_in, grads, basis_out, precision=la...  15.3 us
    dot_general x2, matrix products, precondition(): jnp.einsum('tia,qtab,tjb->qtij', basis_in, scaled, basis_out, precision=l...  13.3 us
    gather x1, local copies, waits for them, and re-layouts, on_device(): ordered = jnp.take(ready, query_order, axis=0)  7.05 us
    all_gather x1, local copies, waits for them, and re-layouts, on_device(): gathered = lax.all_gather(queries, 'seq', axis=0, tiled=True)  5.61 us
    convert_element_type x1, local copies, waits for them, and re-layouts, on_device(): ready = precondition(grads, basis_in, basis_out, values).reshape(gathered...  4.1 us
  transfers between devices with their start and end apart: 2, of which 2 were waited for; matrix products, arithmetic and copies ran while one was open for 4% of the time, Pallas kernels for 0%

commit v1 on v0

--- a/solution.py
+++ b/solution.py
@@ -25,13 +25,13 @@
     basis_in = jnp.take(eig_in, model_ids, axis=0)
     basis_out = jnp.take(eig_out, model_ids, axis=0)
     values = jnp.take(eig_val, model_ids, axis=0)
-    gathered = lax.all_gather(queries, "seq", axis=0, tiled=True)
-    grads = gathered.reshape(gathered.shape[0], slots_here, A, B)
+    grads = queries.reshape(queries.shape[0], slots_here, A, B)
     ready = (
         precondition(grads, basis_in, basis_out, values)
-        .reshape(gathered.shape[0], slots_here * width)
+        .reshape(queries.shape[0], slots_here * width)
         .astype(jnp.bfloat16)
     )
+    ready = lax.all_gather(ready, "seq", axis=0, tiled=True)
     ordered = jnp.take(ready, query_order, axis=0)
     return lax.psum_scatter(
         lax.dot_general(

time: 167 us -> 114 us (0.68)
  waiting for transfers between devices: 97.3 us -> 67.5 us
  matrix products: 31 us -> 13.3 us
  local copies, waits for them, and re-layouts: 23.3 us -> 19.1 us
    all_gather x1, waiting for transfers between devices: 77.9 us -> 48.5 us  [on_device(): ready = lax.all_gather(ready, 'seq', axis=0, tiled=True)]
    dot_general x2, matrix products: 15.3 us -> 5.53 us  [precondition(): jnp.einsum('tai,qtab,tbj->qtij', basis_in, grads, basis_out, precision=la...]
    dot_general x2, matrix products: 13.3 us -> 5.45 us  [precondition(): jnp.einsum('tia,qtab,tjb->qtij', basis_in, scaled, basis_out, precision=l...]
    all_gather x1 -> x0, local copies, waits for them, and re-layouts: 5.61 us -> none  [on_device(): gathered = lax.all_gather(queries, 'seq', axis=0, tiled=True)]
    reshape x0 -> x1, local copies, waits for them, and re-layouts: none -> 3.12 us  [on_device(): grads = queries.reshape(queries.shape[0], slots_here, A, B)]
    convert_element_type x1 -> x2, local copies, waits for them, and re-layouts: 4.1 us -> 2.29 us  [on_device(): ready = precondition(grads, basis_in, basis_out, values).reshape(queries....]
  transfers between devices with their start and end apart: 2 -> 2, of which waited for: 2 -> 2; matrix products, arithmetic and copies ran while one was open for 4% -> 0% of each run, Pallas kernels for 0% -> 0%
where the time goes in v1:
time: 114 us
  waiting for transfers between devices  67.5 us (59%)
  local copies, waits for them, and re-layouts  19.1 us (17%)
  between operations  13.5 us (12%)
  matrix products  13.3 us (12%)
    all_gather x1, waiting for transfers between devices, on_device(): ready = lax.all_gather(ready, 'seq', axis=0, tiled=True)  48.5 us
    reduce_scatter x1, waiting for transfers between devices, on_device(): lax.psum_scatter(lax.dot_general(store, ordered, (((1,), (1,)), ((), ()))...  18.9 us
    gather x1, local copies, waits for them, and re-layouts, on_device(): ordered = jnp.take(ready, query_order, axis=0)  7.04 us
    dot_general x2, matrix products, precondition(): jnp.einsum('tai,qtab,tbj->qtij', basis_in, grads, basis_out, precision=la...  5.53 us
    dot_general x2, matrix products, precondition(): jnp.einsum('tia,qtab,tjb->qtij', basis_in, scaled, basis_out, precision=l...  5.45 us
    reshape x1, local copies, waits for them, and re-layouts, on_device(): grads = queries.reshape(queries.shape[0], slots_here, A, B)  3.12 us
    dot_general x1, matrix products, on_device(): lax.dot_general(store, ordered, (((1,), (1,)), ((), ())), preferred_eleme...  2.34 us
    convert_element_type x2, local copies, waits for them, and re-layouts, on_device(): ready = precondition(grads, basis_in, basis_out, values).reshape(queries....  2.29 us
  transfers between devices with their start and end apart: 2, of which 2 were waited for; matrix products, arithmetic and copies ran while one was open for 0% of the time, Pallas kernels for 0%

profile of v1, /device:TPU:0, one launch (start us, length us, event | category | flops | bytes accessed | tf_op | source)
XLA Modules:
  0.0 113.8 jit_solution(18207408087478063419)
XLA Ops:
  6.5 0.0 copy-start
  6.5 0.0 all-gather.2.cloned.1.call-start
  6.6 1.4 %gather_fusion = s32[2]{0:T(128)S(1)} fusion(s32[8]{0:T(128)} %param.9, s32[1024]{0:T(1024)S(1)} %pad_clamp_fusion.2), kind=kCustom, calls=%fused_computation | custom fusion | bytes 24 | tf_op jit(solution)/shard_map/jit(_take)/gather | solution.py:24
  8.0 3.1 %reshape.67 = f32[64,2,32,64]{3,2,1,0:T(8,128)} reshape(f32[64,4096]{1,0:T(8,128)} %param.8) | data formatting | bytes 2097152 | tf_op jit(solution)/shard_map/reshape | solution.py:28
  11.2 1.5 %gather_fusion.1 = f32[2,32,32]{2,1,0:T(8,128)S(1)} fusion(f32[8,32,32]{2,1,0:T(8,128)} %param.10, s32[1024]{0:T(1024)S(1)} %pad_clamp_fusion.1), kind=kCustom, calls=%fused_computation.1 | custom fusion | bytes 16392 | tf_op jit(solution)/shard_map/jit(_take)/gather | solution.py:25
  12.6 1.5 %gather_fusion.2 = f32[2,64,64]{2,1,0:T(8,128)S(1)} fusion(f32[8,64,64]{2,1,0:T(8,128)} %param.11, s32[1024]{0:T(1024)S(1)} %pad_clamp_fusion.1), kind=kCustom, calls=%fused_computation.2 | custom fusion | bytes 65544 | tf_op jit(solution)/shard_map/jit(_take)/gather | solution.py:26
  14.1 1.5 %gather_fusion.3 = f32[2,32,64]{2,1,0:T(8,128)S(1)} fusion(f32[8,32,64]{2,1,0:T(8,128)} %param.12, s32[1024]{0:T(1024)S(1)} %pad_clamp_fusion.1), kind=kCustom, calls=%fused_computation.3 | custom fusion | bytes 32776 | tf_op jit(solution)/shard_map/jit(_take)/gather | solution.py:27
  15.6 0.1 select_add_fusion
  15.7 3.5 %fusion.6 = f32[2,32,64,64]{3,1,2,0:T(8,128)S(1)} fusion(f32[64,2,32,64]{3,2,1,0:T(8,128)} %reshape.67, f32[2,32,32]{2,1,0:T(8,128)S(1)} %gather_fusion.1, pred[2]{0:T(512)(128)(4,1)S(1)} %compare_and_fusion), kind=kOutput, calls=%fused_computation.11 | convolution fusion | flops 100665344 | bytes 2105346 | tf_op jit(solution)/shard_map/tai,qtab,tbj->qtij/dot_general | solution.py:11
  19.2 2.0 %fusion.2 = f32[2,64,32,64]{3,2,1,0:T(8,128)S(1)} fusion(f32[2,32,64,64]{3,1,2,0:T(8,128)S(1)} %fusion.6, f32[2,64,64]{2,1,0:T(8,128)S(1)} %gather_fusion.2, pred[2]{0:T(512)(128)(4,1)S(1)} %compare_and_fusion), kind=kOutput, calls=%fused_computation.7 | convolution fusion | flops 201334784 | bytes 2129922 | tf_op jit(solution)/shard_map/tai,qtab,tbj->qtij/dot_general | solution.py:11
  21.2 2.0 %fusion.12 = f32[64,2,64,32]{2,3,0,1:T(8,128)S(1)} fusion(f32[2,64,32,64]{3,2,1,0:T(8,128)S(1)} %fusion.2, f32[2,32,64]{2,1,0:T(8,128)S(1)} %select_add_fusion, f32[2,32,32]{2,1,0:T(8,128)S(1)} %gather_fusion.1, pred[2]{0:T(512)(128)(4,1)S(1)} %compare_and_fusion), kind=kOutput, calls=%fused_computation.17 | convolution fusion | flops 100927488 | bytes 2121730 | tf_op jit(solution)/shard_map/tia,qtab,tjb->qtij/dot_general | solution.py:15
  23.2 3.5 %fusion.18 = bf16[64,2,32,64]{3,0,2,1:T(8,128)(2,1)S(1)} fusion(f32[64,2,64,32]{2,3,0,1:T(8,128)S(1)} %fusion.12, f32[2,64,64]{2,1,0:T(8,128)S(1)} %gather_fusion.2, pred[2]{0:T(512)(128)(4,1)S(1)} %compare_and_fusion), kind=kOutput, calls=%fused_computation.19 | convolution fusion | flops 201596928 | bytes 1605634 | tf_op jit(solution)/shard_map/tia,qtab,tjb->qtij/dot_general | solution.py:15
  26.7 0.0 copy-start.1
  26.7 0.7 copy.14
  27.4 1.6 %convert_element_type.11 = bf16[64,4096]{1,0:T(8,128)(2,1)} reshape(bf16[64,2,32,64]{3,2,1,0:T(8,128)(2,1)S(1)} %copy.14) | data formatting | bytes 1048576 | tf_op jit(solution)/shard_map/convert_element_type | solution.py:32
  29.0 0.0 all-gather.2.cloned.1.call-update
  29.0 0.2 reduce-scatter.4.cloned.1.call-start
  29.3 48.5 %all-gather.2.cloned.1.call-done = bf16[256,4096]{1,0:T(8,128)(2,1)} async-done(((bf16[64,4096]{1,0:T(8,128)(2,1)}), bf16[256,4096]{1,0:T(8,128)(2,1)}) %all-gather.2.cloned.1.call-update) | async-done | bytes 2097168 | tf_op jit(solution)/shard_map/all_gather | solution.py:34
  77.8 7.0 %gather_fusion.4 = bf16[256,4096]{1,0:T(8,128)(2,1)} fusion(bf16[256,4096]{1,0:T(8,128)(2,1)} %all-gather.2.cloned.1.call-done, s32[1024]{0:T(1024)S(1)} %pad_clamp_fusion), kind=kCustom, calls=%fused_computation.4 | custom fusion | bytes 4195328 | tf_op jit(solution)/shard_map/jit(_take)/gather | solution.py:35
  84.8 0.0 copy-done
  84.9 2.3 %fusion.21 = f32[256,256]{0,1:T(8,128)S(1)} fusion(bf16[256,4096]{1,0:T(8,128)(2,1)S(1)} %copy-done, bf16[256,4096]{1,0:T(8,128)(2,1)} %gather_fusion.4, pred[256]{0:T(512)(128)(4,1)S(1)} %compare_and_fusion.1), kind=kOutput, calls=%fused_computation.20 | convolution fusion | flops 537919488 | bytes 4456704 | tf_op jit(solution)/shard_map/dot_general | solution.py:37
  87.2 0.8 copy.21
  88.0 0.0 reduce-scatter.4.cloned.1.call-update
  88.1 18.9 %reduce-scatter.4.cloned.1.call-done = f32[64,256]{1,0:T(8,128)} async-done(((f32[256,256]{1,0:T(8,128)}), f32[64,256]{1,0:T(8,128)}) %reduce-scatter.4.cloned.1.call-update) | async-done | bytes 65552 | tf_op jit(solution)/shard_map/reduce_scatter | solution.py:36
  (9 shorter events, 0.1 us)
Async XLA Ops:
  6.5 78.3 %copy-start = (bf16[256,4096]{1,0:T(8,128)(2,1)S(1)}, bf16[256,4096]{1,0:T(8,128)(2,1)}, u32[]{:S(2)}) copy-start(bf16[256,4096]{1,0:T(8,128)(2,1)} %param.7) | copy-start | bytes 6291460
  6.5 71.3 %all-gather.2.cloned.1.call-start = ((), (), s32[]{:S(2)}) async-start(), calls=%async_computation.1 | async-start | bytes 2621440 | tf_op jit(solution)/shard_map/all_gather | solution.py:34
  26.7 2.6 %copy-start.1 = (s32[256]{0:T(256)S(1)}, s32[256]{0:T(256)}, u32[]{:S(2)}) copy-start(s32[256]{0:T(256)} %param.13) | copy-start | bytes 3076
  29.0 78.0 %reduce-scatter.4.cloned.1.call-start = ((), (), s32[]{:S(2)}) async-start(), calls=%async_computation.2 | async-start | bytes 327680 | tf_op jit(solution)/shard_map/reduce_scatter | solution.py:36
Sparse Core Ops, SparseCore 0:
  29.1 48.6 all-gather.1
  88.2 18.7 reduce-scatter.3

commit v2 on v1

v2 whole, which is shorter than its diff:
```python
import functools

import jax
import jax.numpy as jnp
from jax import lax
from jax.experimental import pallas as pl
from jax.experimental.pallas import tpu as pltpu
from jax.sharding import PartitionSpec as P

A = 32
B = 64
WIDTH = A * B
LANES = 2 * B
PAIRS = A // 2
CHUNK = 16
GROUP = 4
MESH = pl.DeviceIdType.MESH
EXACT = lax.Precision.HIGHEST


def split(x):
    high = x.astype(jnp.bfloat16)
    return high, (x - high.astype(jnp.float32)).astype(jnp.bfloat16)


def kernel(
    sizes, owner, store, queries, eig_in, eig_out, eig_val, order, out,
    raw, held, ready, mix_in, mix_back, both, small, inverse, wide, narrow, total, stage, sums, perm,
    raw_sem, held_sem, up_sem, down_sem, side_sem, arrive, part_sem, part_arrive,
):
    n_parts, n_seq, n_layer = sizes
    rows = queries.shape[0]
    n_chunks = rows // CHUNK
    block = out.shape[0]
    mine = lax.axis_index("parts")
    here = lax.axis_index("seq")
    layer = lax.axis_index("layer")
    other = 1 - mine

    barrier = pltpu.get_barrier_semaphore()

    def greet(**where):
        pl.semaphore_signal(barrier, inc=1, device_id=where, device_id_type=MESH)

    @pl.when(here > 0)
    def _():
        greet(seq=here - 1)

    @pl.when(here < n_seq - 1)
    def _():
        greet(seq=here + 1)

    greet(parts=other)
    for step in range(1, n_layer):
        greet(layer=lax.rem(layer + step, n_layer))

    def fetch(n):
        slot = jnp.where(n < n_chunks, mine, other)
        piece = (
            pl.ds(pl.multiple_of(lax.rem(n, n_chunks) * CHUNK, CHUNK), CHUNK),
            pl.ds(pl.multiple_of(slot * WIDTH, WIDTH), WIDTH),
        )
        return pltpu.make_async_copy(queries.at[piece], raw.at[n], raw_sem.at[n])

    for n in range(2 * n_chunks):
        fetch(n).start()
    fetch_store = pltpu.make_async_copy(store, held, held_sem)
    fetch_store.start()

    def setup(slot):
        model = owner[layer * 2 + slot]
        basis_in = eig_in[model]
        basis_out = eig_out[model]
        spread = (
            lax.shift_right_logical(lax.broadcasted_iota(jnp.int32, (A, WIDTH), 1), 6)
            == lax.broadcasted_iota(jnp.int32, (A, WIDTH), 0)
        ).astype(jnp.float32)
        mix_in[slot] = jnp.dot(basis_in, spread, precision=EXACT, preferred_element_type=jnp.float32)
        mix_back[slot] = lax.dot_general(
            basis_in, spread, (((0,), (0,)), ((), ())), precision=EXACT,
            preferred_element_type=jnp.float32,
        )
        twice = (
            lax.broadcasted_iota(jnp.int32, (B, LANES), 1) & (B - 1)
            == lax.broadcasted_iota(jnp.int32, (B, LANES), 0)
        ).astype(jnp.float32)
        both[slot] = jnp.zeros(both.shape[1:], both.dtype)
        small[slot] = jnp.zeros(small.shape[1:], small.dtype)
        for way, dims in enumerate((1, 0)):
            doubled = lax.dot_general(
                basis_out, twice, (((dims,), (0,)), ((), ())), precision=EXACT,
                preferred_element_type=jnp.float32,
            )
            high, low = split(doubled)
            for at in range(2):
                column = pl.ds(at * LANES, LANES)
                both[slot, way, pl.ds(at * B, B), column] = high
                both[slot, way, pl.ds(LANES + at * B, B), column] = high
                small[slot, way, pl.ds(at * B, B), column] = low
        values = jnp.dot(
            1.0 / (eig_val[model] + 0.1), twice, precision=EXACT, preferred_element_type=jnp.float32
        )
        pair = lax.broadcasted_iota(jnp.int32, (PAIRS, A), 0) * 2
        slots = lax.broadcasted_iota(jnp.int32, (PAIRS, A), 1)
        even = jnp.dot((slots == pair).astype(jnp.float32), values, precision=EXACT,
                       preferred_element_type=jnp.float32)
        odd = jnp.dot((slots == pair + 1).astype(jnp.float32), values, precision=EXACT,
                      preferred_element_type=jnp.float32)
        lane = lax.broadcasted_iota(jnp.int32, (PAIRS, LANES), 1)
        inverse[slot] = jnp.where(lane < B, even, odd)

    def rotate(x, slot, way):
        high, low = split(x)
        wide[...] = jnp.dot(
            jnp.concatenate([high, low], axis=1), both[slot, way], preferred_element_type=jnp.float32
        ) + jnp.dot(high, small[slot, way], preferred_element_type=jnp.float32)

    def mix(weights, slot, first):
        sums_of = [None] * GROUP
        for a in range(A):
            y = wide[pl.ds(CHUNK * (a // 2), CHUNK), pl.ds(LANES * (a % 2), LANES)]
            for g in range(GROUP):
                w = weights[slot, pl.ds(a, 1), pl.ds(pl.multiple_of((first + g) * LANES, LANES), LANES)]
                term = w * y
                sums_of[g] = term if a == 0 else sums_of[g] + term
        return sums_of

    def at_rows(source, k):
        return pl.ds(pl.multiple_of(source * rows + k * CHUNK, CHUNK), CHUNK)

    def precondition(slot, n, k):
        x = jnp.concatenate(
            [raw[n, :, pl.ds(c * LANES, LANES)] for c in range(PAIRS)], axis=0
        )
        rotate(x, slot, 0)

        def inner(i, _):
            for g, value in enumerate(mix(mix_in, slot, i * GROUP)):
                pair = i * GROUP + g
                narrow[pl.ds(pl.multiple_of(pair * CHUNK, CHUNK), CHUNK), :] = (
                    value * inverse[slot, pl.ds(pair, 1), :]
                )
            return 0

        lax.fori_loop(0, PAIRS // GROUP, inner, 0)
        rotate(narrow[...], slot, 1)

        def outer(i, _):
            for g, value in enumerate(mix(mix_back, slot, i * GROUP)):
                column = pl.ds(pl.multiple_of((i * GROUP + g) * LANES, LANES), LANES)
                ready[slot, at_rows(here, k), column] = value.astype(jnp.bfloat16)
            return 0

        lax.fori_loop(0, PAIRS // GROUP, outer, 0)

    def send(source, k, sems, **where):
        piece = ready.at[mine, at_rows(source, k), :]
        return pltpu.make_async_remote_copy(
            src_ref=piece, dst_ref=piece, send_sem=sems.at[source, k],
            recv_sem=arrive.at[mine, source, k], device_id=where, device_id_type=MESH,
        )

    def to_up(source, k):
        return send(source, k, up_sem, seq=here + 1)

    def to_down(source, k):
        return send(source, k, down_sem, seq=here - 1)

    def to_side(source, k):
        return send(source, k, side_sem, parts=other)

    def await_piece(slot, source, k):
        piece = ready.at[slot, at_rows(source, k), :]
        pltpu.make_async_remote_copy(
            src_ref=piece, dst_ref=piece, send_sem=side_sem.at[source, k],
            recv_sem=arrive.at[slot, source, k], device_id={"parts": other}, device_id_type=MESH,
        ).wait_recv()

    def pass_on(distance, k):
        below, above = here - distance, here + distance

        @pl.when(below >= 0)
        def _():
            await_piece(mine, below, k)

            @pl.when(here < n_seq - 1)
            def _():
                to_up(below, k).start()

            to_side(below, k).start()

        @pl.when(above < n_seq)
        def _():
            await_piece(mine, above, k)

            @pl.when(here > 0)
            def _():
                to_down(above, k).start()

            to_side(above, k).start()

    n_greetings = (
        jnp.where(here > 0, 1, 0) + jnp.where(here < n_seq - 1, 1, 0) + n_layer
    )

    def job(n, _):
        k = lax.rem(n, n_chunks)
        slot = jnp.where(n < n_chunks, mine, other)

        @pl.when(k == 0)
        def _():
            setup(slot)

        fetch(n).wait()
        precondition(slot, n, k)

        @pl.when(n == 0)
        def _():
            pl.semaphore_wait(barrier, n_greetings)

        @pl.when(n < n_chunks)
        def _():
            @pl.when(here < n_seq - 1)
            def _():
                to_up(here, k).start()

            @pl.when(here > 0)
            def _():
                to_down(here, k).start()

        @pl.when(n >= n_chunks)
        def _():
            pass_on(1, k)

        return 0

    lax.fori_loop(0, 2 * n_chunks, job, 0)

    which = lax.broadcasted_iota(jnp.int32, perm.shape, 0)
    perm[...] = (which == order[...].reshape(1, perm.shape[1])).astype(jnp.bfloat16)

    def relay(n, _):
        pass_on(2 + n // n_chunks, lax.rem(n, n_chunks))
        return 0

    lax.fori_loop(0, (n_seq - 2) * n_chunks, relay, 0)

    def score(slot):
        return lax.dot_general(
            held[:, pl.ds(pl.multiple_of(slot * WIDTH, WIDTH), WIDTH)], ready[slot],
            (((1,), (1,)), ((), ())), preferred_element_type=jnp.float32,
        )

    fetch_store.wait()
    total[...] = score(mine)

    def each_source(do):
        def body(n, _):
            source = n // n_chunks

            @pl.when(source != here)
            def _():
                do(source, lax.rem(n, n_chunks))

            return 0

        lax.fori_loop(0, n_seq * n_chunks, body, 0)

    each_source(lambda source, k: await_piece(other, source, k))
    total[...] += score(other)

    stage[...] = total[...].astype(jnp.bfloat16)

    def part(step):
        to = lax.rem(layer + step, n_layer)
        return pltpu.make_async_remote_copy(
            src_ref=stage.at[pl.ds(pl.multiple_of(to * block, CHUNK), block), :],
            dst_ref=sums.at[step - 1], send_sem=part_sem.at[step - 1],
            recv_sem=part_arrive.at[step - 1], device_id={"layer": to}, device_id_type=MESH,
        )

    for step in range(1, n_layer):
        part(step).start()

    each_source(lambda source, k: to_side(source, k).wait_send())

    def drain(n, _):
        source, k = n // n_chunks, lax.rem(n, n_chunks)

        @pl.when((source <= here) & (here < n_seq - 1))
        def _():
            to_up(source, k).wait_send()

        @pl.when((source >= here) & (here > 0))
        def _():
            to_down(source, k).wait_send()

        return 0

    lax.fori_loop(0, n_seq * n_chunks, drain, 0)

    result = total[pl.ds(pl.multiple_of(layer * block, CHUNK), block), :]
    for step in range(1, n_layer):
        part(step).wait_recv()
        result = result + sums[step - 1].astype(jnp.float32)
    high, low = split(result)
    lowest = (result - high.astype(jnp.float32) - low.astype(jnp.float32)).astype(jnp.bfloat16)
    out[...] = sum(
        jnp.dot(piece, perm[...], preferred_element_type=jnp.float32) for piece in (lowest, low, high)
    )
    for step in range(1, n_layer):
        part(step).wait_send()


def on_device(sizes, store, queries, owner, eig_in, eig_out, eig_val, query_order):
    n_parts, n_seq, n_layer = sizes
    rows = queries.shape[0]
    n_queries = rows * n_seq
    n_store = store.shape[0]
    n_chunks = rows // CHUNK
    slots = store.shape[1] // WIDTH
    assert slots == 2 and n_parts == 2 and rows % CHUNK == 0
    block = n_store // n_layer
    vmem = pl.BlockSpec(memory_space=pltpu.VMEM)
    anywhere = pl.BlockSpec(memory_space=pl.ANY)
    f32, bf16 = jnp.float32, jnp.bfloat16
    dma = pltpu.SemaphoreType.DMA
    return pl.pallas_call(
        functools.partial(kernel, sizes),
        out_shape=jax.ShapeDtypeStruct((block, n_queries), f32),
        in_specs=[pl.BlockSpec(memory_space=pltpu.SMEM), anywhere, anywhere, vmem, vmem, vmem, vmem],
        out_specs=vmem,
        scratch_shapes=[
            pltpu.VMEM((slots * n_chunks, CHUNK, WIDTH), f32),
            pltpu.VMEM(store.shape, bf16),
            pltpu.VMEM((slots, n_queries, WIDTH), bf16),
            pltpu.VMEM((slots, A, WIDTH), f32),
            pltpu.VMEM((slots, A, WIDTH), f32),
            pltpu.VMEM((slots, 2, 2 * LANES, 2 * LANES), bf16),
            pltpu.VMEM((slots, 2, LANES, 2 * LANES), bf16),
            pltpu.VMEM((slots, PAIRS, LANES), f32),
            pltpu.VMEM((PAIRS * CHUNK, 2 * LANES), f32),
            pltpu.VMEM((PAIRS * CHUNK, LANES), f32),
            pltpu.VMEM((n_store, n_queries), f32),
            pltpu.VMEM((n_store, n_queries), bf16),
            pltpu.VMEM((n_layer - 1, block, n_queries), bf16),
            pltpu.VMEM((n_queries, n_queries), bf16),
            dma((slots * n_chunks,)),
            dma,
            dma((n_seq, n_chunks)),
            dma((n_seq, n_chunks)),
            dma((n_seq, n_chunks)),
            dma((slots, n_seq, n_chunks)),
            dma((n_layer - 1,)),
            dma((n_layer - 1,)),
        ],
        compiler_params=pltpu.CompilerParams(
            collective_id=0, has_side_effects=True, vmem_limit_bytes=48 * 1024 * 1024
        ),
        name="gather_score",
    )(owner, store, queries, eig_in, eig_out, eig_val, query_order)


def solution(mesh):
    sizes = tuple(mesh.shape[axis] for axis in ("parts", "seq", "layer"))
    in_specs = (P(("parts", "seq"), "layer"), P("seq", "layer"), P(), P(), P(), P(), P())
    out_specs = P(("parts", "seq", "layer"), None)
    return jax.shard_map(
        functools.partial(on_device, sizes), mesh=mesh, in_specs=in_specs, out_specs=out_specs,
        check_vma=False,
    )
```

time: 114 us -> 43.9 us (0.39)
  waiting for transfers between devices: 67.5 us -> 0 us
  Pallas kernels: 0 us -> 36.1 us
  between operations: 13.5 us -> 0.02 us
  matrix products: 13.3 us -> 0 us
  local copies, waits for them, and re-layouts: 19.1 us -> 7.54 us
    all_gather x1 -> x0, waiting for transfers between devices: 48.5 us -> none  [on_device(): ready = lax.all_gather(ready, 'seq', axis=0, tiled=True)]
    pallas_call x0 -> x1, Pallas kernels: none -> 36.1 us  [on_device(): pl.pallas_call(functools.partial(kernel, sizes), out_shape=jax.ShapeDtype...]
    reduce_scatter x1 -> x0, waiting for transfers between devices: 18.9 us -> none  [on_device(): lax.psum_scatter(lax.dot_general(store, ordered, (((1,), (1,)), ((), ()))...]
    dot_general x5 -> x0, matrix products: 13.3 us -> none  [the longest x2 5.53 us: precondition(): jnp.einsum('tai,qtab,tbj->qtij', basis_in, grads, basis_out, precision=la...]
    gather x5 -> x0, local copies, waits for them, and re-layouts: 12.9 us -> none  [the longest x1 7.04 us: on_device(): ordered = jnp.take(ready, query_order, axis=0)]
    unnamed x5 -> x15, local copies, waits for them, and re-layouts: 0.84 us -> 7.54 us
    reshape x1 -> x0, local copies, waits for them, and re-layouts: 3.12 us -> none  [on_device(): grads = queries.reshape(queries.shape[0], slots_here, A, B)]
    convert_element_type x2 -> x0, local copies, waits for them, and re-layouts: 2.29 us -> none  [on_device(): ready = precondition(grads, basis_in, basis_out, values).reshape(queries....]
  transfers between devices with their start and end apart: 2 -> 0, of which waited for: 2 -> 0; matrix products, arithmetic and copies ran while one was open for 0% -> 0% of each run, Pallas kernels for 0% -> 0%
where the time goes in v2:
time: 43.9 us; the launch traced here: 43.7 us
  Pallas kernels  36.1 us (82%)
  local copies, waits for them, and re-layouts  7.54 us (17%)
    pallas_call x1, Pallas kernels, on_device(): pl.pallas_call(functools.partial(kernel, sizes), out_shape=jax.ShapeDtype...  36.1 us
    unnamed x15, local copies, waits for them, and re-layouts  7.54 us

profile of v2, /device:TPU:0, one launch (start us, length us, event | category | flops | bytes accessed | tf_op | source)
XLA Modules:
  0.0 43.7 jit_solution(10550512342917554856)
XLA Ops:
  0.0 0.0 copy-start
  0.0 1.6 %copy-done = bf16[256,4096]{1,0:T(8,128)(2,1)S(1)} copy-done((bf16[256,4096]{1,0:T(8,128)(2,1)S(1)}, bf16[256,4096]{1,0:T(8,128)(2,1)}, u32[]{:S(2)}) %copy-start) | copy-done | bytes 2097176
  1.6 0.0 copy-start.1
  1.6 1.2 %copy-done.1 = f32[64,4096]{1,0:T(8,128)S(1)} copy-done((f32[64,4096]{1,0:T(8,128)S(1)}, f32[64,4096]{1,0:T(8,128)}, u32[]{:S(2)}) %copy-start.1) | copy-done | bytes 1048600
  2.8 0.0 copy-start.2
  2.8 0.9 %copy-done.2 = f32[8,64,64]{2,1,0:T(8,128)S(1)} copy-done((f32[8,64,64]{2,1,0:T(8,128)S(1)}, f32[8,64,64]{2,1,0:T(8,128)}, u32[]{:S(2)}) %copy-start.2) | copy-done | bytes 131096
  3.8 0.0 copy-start.3
  3.8 0.9 %copy-done.3 = f32[8,32,32]{2,1,0:T(8,128)S(1)} copy-done((f32[8,32,32]{2,1,0:T(8,128)S(1)}, f32[8,32,32]{2,1,0:T(8,128)}, u32[]{:S(2)}) %copy-start.3) | copy-done | bytes 32792
  4.7 0.0 copy-start.4
  4.7 0.9 %copy-done.4 = f32[8,32,64]{2,1,0:T(8,128)S(1)} copy-done((f32[8,32,64]{2,1,0:T(8,128)S(1)}, f32[8,32,64]{2,1,0:T(8,128)}, u32[]{:S(2)}) %copy-start.4) | copy-done | bytes 65560
  5.6 0.0 copy-start.5
  5.6 0.7 %copy-done.5 = s32[256]{0:T(256)S(1)} copy-done((s32[256]{0:T(256)S(1)}, s32[256]{0:T(256)}, u32[]{:S(2)}) %copy-start.5) | copy-done | bytes 1048
  6.3 0.0 copy-start.6
  6.3 0.7 %copy-done.6 = s32[8]{0:T(128)S(1)} copy-done((s32[8]{0:T(128)S(1)}, s32[8]{0:T(128)}, u32[]{:S(2)}) %copy-start.6) | copy-done | bytes 56
  6.9 36.1 %gather_score.1 = f32[64,256]{1,0:T(8,128)S(1)} custom-call(s32[8]{0:T(128)S(1)} %copy-done.6, bf16[256,4096]{1,0:T(8,128)(2,1)S(1)} %copy-done, f32[64,4096]{1,0:T(8,128)S(1)} %copy-done.1, f32[8,32,32]{2,1,0:T(8,128)S(1)} %copy-done.3, f32[8,64,64]{2,1,0:T(8,128)S(1)} %copy-done.2, f32[8,32,64]{2,1,0:T(8,128)S(1)} %copy-done.4, s32[256]{0:T(256)S(1)} %copy-done.5), custom_call_target="tpu_custom_call" | custom-call | tf_op jit(solution)/shard_map/gather_score/pallas_call | solution.py:328
  43.0 0.6 %copy.9 = f32[64,256]{1,0:T(8,128)} copy(f32[64,256]{1,0:T(8,128)S(1)} %gather_score.1) | data formatting | bytes 131072
Async XLA Ops:
  0.0 1.6 %copy-start = (bf16[256,4096]{1,0:T(8,128)(2,1)S(1)}, bf16[256,4096]{1,0:T(8,128)(2,1)}, u32[]{:S(2)}) copy-start(bf16[256,4096]{1,0:T(8,128)(2,1)} %store.1) | copy-start | bytes 6291460
  1.6 1.2 %copy-start.1 = (f32[64,4096]{1,0:T(8,128)S(1)}, f32[64,4096]{1,0:T(8,128)}, u32[]{:S(2)}) copy-start(f32[64,4096]{1,0:T(8,128)} %queries.1) | copy-start | bytes 3145732
  2.8 0.9 %copy-start.2 = (f32[8,64,64]{2,1,0:T(8,128)S(1)}, f32[8,64,64]{2,1,0:T(8,128)}, u32[]{:S(2)}) copy-start(f32[8,64,64]{2,1,0:T(8,128)} %eig_out.1) | copy-start | bytes 393220
  3.8 0.9 %copy-start.3 = (f32[8,32,32]{2,1,0:T(8,128)S(1)}, f32[8,32,32]{2,1,0:T(8,128)}, u32[]{:S(2)}) copy-start(f32[8,32,32]{2,1,0:T(8,128)} %eig_in.1) | copy-start | bytes 98308
  4.7 0.9 %copy-start.4 = (f32[8,32,64]{2,1,0:T(8,128)S(1)}, f32[8,32,64]{2,1,0:T(8,128)}, u32[]{:S(2)}) copy-start(f32[8,32,64]{2,1,0:T(8,128)} %eig_val.1) | copy-start | bytes 196612
  5.6 0.7 %copy-start.5 = (s32[256]{0:T(256)S(1)}, s32[256]{0:T(256)}, u32[]{:S(2)}) copy-start(s32[256]{0:T(256)} %order.1) | copy-start | bytes 3076
  6.3 0.7 %copy-start.6 = (s32[8]{0:T(128)S(1)}, s32[8]{0:T(128)}, u32[]{:S(2)}) copy-start(s32[8]{0:T(128)} %owner.1) | copy-start | bytes 100

commit v3 on v2

--- a/solution.py
+++ b/solution.py
@@ -24,8 +24,8 @@
 
 
 def kernel(
-    sizes, owner, store, queries, eig_in, eig_out, eig_val, order, out,
-    raw, held, ready, mix_in, mix_back, both, small, inverse, wide, narrow, total, stage, sums, perm,
+    sizes, owner_at, store, queries, eig_in_at, eig_out_at, eig_val_at, order_at, out,
+    owner, eig_in, eig_out, eig_val, order, small_sem, raw, held, ready, mix_in, mix_back, both, small, inverse, wide, narrow, total, stage, sums, perm,
     raw_sem, held_sem, up_sem, down_sem, side_sem, arrive, part_sem, part_arrive,
 ):
     n_parts, n_seq, n_layer = sizes
@@ -62,10 +62,22 @@
         )
         return pltpu.make_async_copy(queries.at[piece], raw.at[n], raw_sem.at[n])
 
+    tables = [
+        pltpu.make_async_copy(source, target, small_sem.at[i])
+        for i, (source, target) in enumerate((
+            (owner_at, owner), (eig_in_at, eig_in), (eig_out_at, eig_out), (eig_val_at, eig_val),
+            (order_at, order),
+        ))
+    ]
+    for table in tables:
+        table.start()
     for n in range(2 * n_chunks):
         fetch(n).start()
     fetch_store = pltpu.make_async_copy(store, held, held_sem)
     fetch_store.start()
+
+    for table in tables:
+        table.wait()
 
     def setup(slot):
         model = owner[layer * 2 + slot]
@@ -328,9 +340,15 @@
     return pl.pallas_call(
         functools.partial(kernel, sizes),
         out_shape=jax.ShapeDtypeStruct((block, n_queries), f32),
-        in_specs=[pl.BlockSpec(memory_space=pltpu.SMEM), anywhere, anywhere, vmem, vmem, vmem, vmem],
+        in_specs=[anywhere] * 7,
         out_specs=vmem,
         scratch_shapes=[
+            pltpu.SMEM(owner.shape, owner.dtype),
+            pltpu.VMEM(eig_in.shape, f32),
+            pltpu.VMEM(eig_out.shape, f32),
+            pltpu.VMEM(eig_val.shape, f32),
+            pltpu.VMEM(query_order.shape, query_order.dtype),
+            dma((5,)),
             pltpu.VMEM((slots * n_chunks, CHUNK, WIDTH), f32),
             pltpu.VMEM(store.shape, bf16),
             pltpu.VMEM((slots, n_queries, WIDTH), bf16),
@@ -355,7 +373,7 @@
             dma((n_layer - 1,)),
         ],
         compiler_params=pltpu.CompilerParams(
-            collective_id=0, has_side_effects=True, vmem_limit_bytes=48 * 1024 * 1024
+            collective_id=0, has_side_effects=True, vmem_limit_bytes=60 * 1024 * 1024
         ),
         name="gather_score",
     )(owner, store, queries, eig_in, eig_out, eig_val, query_order)

time: 43.9 us -> 38.5 us (0.88)
  local copies, waits for them, and re-layouts: 7.54 us -> 1.47 us
  Pallas kernels: 36.1 us -> 36.8 us
    unnamed x15 -> x1, local copies, waits for them, and re-layouts: 7.54 us -> 1.47 us
    pallas_call x1, Pallas kernels: 36.1 us -> 36.8 us  [on_device(): pl.pallas_call(functools.partial(kernel, sizes), out_shape=jax.ShapeDtype...]
where the time goes in v3:
time: 38.5 us; the launch traced here: 38.3 us
  Pallas kernels  36.8 us (96%)
  local copies, waits for them, and re-layouts  1.47 us (4%)
    pallas_call x1, Pallas kernels, on_device(): pl.pallas_call(functools.partial(kernel, sizes), out_shape=jax.ShapeDtype...  36.8 us
    unnamed x1, local copies, waits for them, and re-layouts  1.47 us

profile of v3, /device:TPU:0, one launch (start us, length us, event | category | flops | bytes accessed | tf_op | source)
XLA Modules:
  0.0 38.3 jit_solution(15233428233501953019)
XLA Ops:
  0.0 36.8 %gather_score.1 = f32[64,256]{1,0:T(8,128)} custom-call(s32[8]{0:T(128)} %owner_at.1, bf16[256,4096]{1,0:T(8,128)(2,1)} %store.1, f32[64,4096]{1,0:T(8,128)} %queries.1, f32[8,32,32]{2,1,0:T(8,128)} %eig_in_at.1, f32[8,64,64]{2,1,0:T(8,128)} %eig_out_at.1, f32[8,32,64]{2,1,0:T(8,128)} %eig_val_at.1, s32[256]{0:T(256)} %order_at.1), custom_call_target="tpu_custom_call" | custom-call | tf_op jit(solution)/shard_map/gather_score/pallas_call | solution.py:340
  36.8 1.5 %copy.9 = f32[64,256]{1,0:T(8,128)} copy(f32[64,256]{1,0:T(8,128)} %gather_score.1) | data formatting | bytes 131072

commit v4 on v3

--- a/solution.py
+++ b/solution.py
@@ -13,7 +13,9 @@
 LANES = 2 * B
 PAIRS = A // 2
 CHUNK = 16
-GROUP = 4
+GROUP = 16
+HALVES = 1
+SPREAD = 2
 MESH = pl.DeviceIdType.MESH
 EXACT = lax.Precision.HIGHEST
 
@@ -26,7 +28,7 @@
 def kernel(
     sizes, owner_at, store, queries, eig_in_at, eig_out_at, eig_val_at, order_at, out,
     owner, eig_in, eig_out, eig_val, order, small_sem, raw, held, ready, mix_in, mix_back, both, small, inverse, wide, narrow, total, stage, sums, perm,
-    raw_sem, held_sem, up_sem, down_sem, side_sem, arrive, part_sem, part_arrive,
+    raw_sem, held_sem, up_sem, down_sem, side_sem, arrive, side_arrive, part_sem, part_arrive,
 ):
     n_parts, n_seq, n_layer = sizes
     rows = queries.shape[0]
@@ -54,10 +56,13 @@
     for step in range(1, n_layer):
         greet(layer=lax.rem(layer + step, n_layer))
 
+    def chunk_of(n):
+        return jnp.where(n < n_chunks, n, 2 * n_chunks - 1 - n)
+
     def fetch(n):
         slot = jnp.where(n < n_chunks, mine, other)
         piece = (
-            pl.ds(pl.multiple_of(lax.rem(n, n_chunks) * CHUNK, CHUNK), CHUNK),
+            pl.ds(pl.multiple_of(chunk_of(n) * CHUNK, CHUNK), CHUNK),
             pl.ds(pl.multiple_of(slot * WIDTH, WIDTH), WIDTH),
         )
         return pltpu.make_async_copy(queries.at[piece], raw.at[n], raw_sem.at[n])
@@ -165,97 +170,100 @@
 
         lax.fori_loop(0, PAIRS // GROUP, outer, 0)
 
-    def send(source, k, sems, **where):
-        piece = ready.at[mine, at_rows(source, k), :]
+    def copy(piece, sem, arrival, **where):
         return pltpu.make_async_remote_copy(
-            src_ref=piece, dst_ref=piece, send_sem=sems.at[source, k],
-            recv_sem=arrive.at[mine, source, k], device_id=where, device_id_type=MESH,
-        )
-
-    def to_up(source, k):
-        return send(source, k, up_sem, seq=here + 1)
-
-    def to_down(source, k):
-        return send(source, k, down_sem, seq=here - 1)
-
-    def to_side(source, k):
-        return send(source, k, side_sem, parts=other)
-
-    def await_piece(slot, source, k):
-        piece = ready.at[slot, at_rows(source, k), :]
-        pltpu.make_async_remote_copy(
-            src_ref=piece, dst_ref=piece, send_sem=side_sem.at[source, k],
-            recv_sem=arrive.at[slot, source, k], device_id={"parts": other}, device_id_type=MESH,
-        ).wait_recv()
-
-    def pass_on(distance, k):
+            src_ref=piece, dst_ref=piece, send_sem=sem, recv_sem=arrival,
+            device_id=where, device_id_type=MESH,
+        )
+
+    def halves(slot, source, k):
+        for h in range(HALVES):
+            yield (
+                ready.at[slot, at_rows(source, k), pl.ds(h * (WIDTH // HALVES), WIDTH // HALVES)],
+                arrive.at[slot, source, k, h],
+            )
+
+    def go_up(slot, source, piece, arrival):
+        @pl.when(here < n_seq - 1)
+        def _():
+            copy(piece, up_sem.at[slot, source], arrival, seq=here + 1).start()
+
+    def go_down(slot, source, piece, arrival):
+        @pl.when(here > 0)
+        def _():
+            copy(piece, down_sem.at[slot, source], arrival, seq=here - 1).start()
+
+    def pass_on(slot, source, k, is_end, ways):
+        for piece, arrival in halves(slot, source, k):
+            copy(piece, side_sem.at[source], arrival, parts=other).wait_recv()
+            for way in ways:
+                way(slot, source, piece, arrival)
+            if slot is mine:
+                @pl.when(jnp.logical_not(is_end & (k == n_chunks - 1)))
+                def _():
+                    copy(piece, side_sem.at[source], side_arrive.at[source], parts=other).start()
+
+    def pass_all(n):
+        distance, k = 1 + n // (n_chunks + 1), lax.rem(n, n_chunks + 1)
         below, above = here - distance, here + distance
-
-        @pl.when(below >= 0)
-        def _():
-            await_piece(mine, below, k)
-
-            @pl.when(here < n_seq - 1)
+        for source, exists, is_end, way in (
+            (below, below >= 0, below == 0, go_up),
+            (above, above < n_seq, above == n_seq - 1, go_down),
+        ):
+            @pl.when(exists & (k < n_chunks))
             def _():
-                to_up(below, k).start()
-
-            to_side(below, k).start()
-
-        @pl.when(above < n_seq)
-        def _():
-            await_piece(mine, above, k)
-
-            @pl.when(here > 0)
+                pass_on(mine, source, k, is_end, (way,))
+
+            @pl.when(exists & (k == n_chunks) & is_end)
             def _():
-                to_down(above, k).start()
-
-            to_side(above, k).start()
+                pass_on(other, source, n_chunks - 1, is_end, (way,))
 
     n_greetings = (
         jnp.where(here > 0, 1, 0) + jnp.where(here < n_seq - 1, 1, 0) + n_layer
     )
 
-    def job(n, _):
-        k = lax.rem(n, n_chunks)
-        slot = jnp.where(n < n_chunks, mine, other)
-
-        @pl.when(k == 0)
-        def _():
-            setup(slot)
-
-        fetch(n).wait()
-        precondition(slot, n, k)
-
-        @pl.when(n == 0)
-        def _():
-            pl.semaphore_wait(barrier, n_greetings)
-
-        @pl.when(n < n_chunks)
-        def _():
-            @pl.when(here < n_seq - 1)
-            def _():
-                to_up(here, k).start()
-
-            @pl.when(here > 0)
-            def _():
-                to_down(here, k).start()
-
-        @pl.when(n >= n_chunks)
-        def _():
-            pass_on(1, k)
-
-        return 0
-
-    lax.fori_loop(0, 2 * n_chunks, job, 0)
-
     which = lax.broadcasted_iota(jnp.int32, perm.shape, 0)
     perm[...] = (which == order[...].reshape(1, perm.shape[1])).astype(jnp.bfloat16)
 
-    def relay(n, _):
-        pass_on(2 + n // n_chunks, lax.rem(n, n_chunks))
+    def job(n, _):
+        slot = jnp.where(n < n_chunks, mine, other)
+        late = n - n_chunks
+        task = jnp.where(n < n_chunks, n, n_chunks + late // SPREAD)
+        due = (n < n_chunks) | ((lax.rem(late, SPREAD) == 0) & (task < 2 * n_chunks))
+
+        @pl.when(n == 1)
+        def _():
+            pl.semaphore_wait(barrier, n_greetings)
+
+        @pl.when((n >= 1) & (n <= n_chunks))
+        def _():
+            for piece, arrival in halves(mine, here, n - 1):
+                go_up(mine, here, piece, arrival)
+                go_down(mine, here, piece, arrival)
+
+        @pl.when((n == n_chunks + 1) & ((here == 0) | (here == n_seq - 1)))
+        def _():
+            for piece, arrival in halves(other, here, n_chunks - 1):
+                go_up(other, here, piece, arrival)
+                go_down(other, here, piece, arrival)
+
+        @pl.when((n >= n_chunks) & (n < n_chunks + (n_seq - 1) * (n_chunks + 1)))
+        def _():
+            pass_all(n - n_chunks)
+
+        @pl.when((n == 0) | (n == n_chunks))
+        def _():
+            setup(slot)
+
+        @pl.when(due)
+        def _():
+            fetch(task).wait()
+            precondition(slot, task, chunk_of(task))
+
         return 0
 
-    lax.fori_loop(0, (n_seq - 2) * n_chunks, relay, 0)
+    n_steps = n_chunks + max((n_seq - 1) * (n_chunks + 1), SPREAD * n_chunks)
+    lax.fori_loop(0, n_steps, job, 0)
 
     def score(slot):
         return lax.dot_general(
@@ -266,19 +274,32 @@
     fetch_store.wait()
     total[...] = score(mine)
 
+    def slab(slot, source, size):
+        return ready.at[slot, pl.ds(pl.multiple_of(source * rows, CHUNK), size), :]
+
     def each_source(do):
-        def body(n, _):
-            source = n // n_chunks
-
+        def body(source, _):
             @pl.when(source != here)
             def _():
-                do(source, lax.rem(n, n_chunks))
+                is_end = (source == 0) | (source == n_seq - 1)
+
+                @pl.when(jnp.logical_not(is_end))
+                def _():
+                    do(source, rows)
+
+                if rows > CHUNK:
+                    @pl.when(is_end)
+                    def _():
+                        do(source, rows - CHUNK)
 
             return 0
 
-        lax.fori_loop(0, n_seq * n_chunks, body, 0)
-
-    each_source(lambda source, k: await_piece(other, source, k))
+        lax.fori_loop(0, n_seq, body, 0)
+
+    def side_slab(slot, source, size):
+        return copy(slab(slot, source, size), side_sem.at[source], side_arrive.at[source], parts=other)
+
+    each_source(lambda source, size: side_slab(other, source, size).wait_recv())
     total[...] += score(other)
 
     stage[...] = total[...].astype(jnp.bfloat16)
@@ -294,22 +315,26 @@
     for step in range(1, n_layer):
         part(step).start()
 
-    each_source(lambda source, k: to_side(source, k).wait_send())
-
-    def drain(n, _):
-        source, k = n // n_chunks, lax.rem(n, n_chunks)
-
-        @pl.when((source <= here) & (here < n_seq - 1))
-        def _():
-            to_up(source, k).wait_send()
-
-        @pl.when((source >= here) & (here > 0))
-        def _():
-            to_down(source, k).wait_send()
+    each_source(lambda source, size: side_slab(mine, source, size).wait_send())
+
+    def drain(source, _):
+        for comes, has_next, sems, where, is_end in (
+            (source <= here, here < n_seq - 1, up_sem, here + 1, source == 0),
+            (source >= here, here > 0, down_sem, here - 1, source == n_seq - 1),
+        ):
+            @pl.when(comes & has_next)
+            def _():
+                copy(slab(mine, source, rows), sems.at[mine, source], arrive.at[mine, source, 0, 0],
+                     seq=where).wait_send()
+
+            @pl.when(comes & has_next & is_end)
+            def _():
+                copy(slab(other, source, CHUNK), sems.at[other, source],
+                     arrive.at[other, source, 0, 0], seq=where).wait_send()
 
         return 0
 
-    lax.fori_loop(0, n_seq * n_chunks, drain, 0)
+    lax.fori_loop(0, n_seq, drain, 0)
 
     result = total[pl.ds(pl.multiple_of(layer * block, CHUNK), block), :]
     for step in range(1, n_layer):
@@ -365,10 +390,11 @@
             pltpu.VMEM((n_queries, n_queries), bf16),
             dma((slots * n_chunks,)),
             dma,
-            dma((n_seq, n_chunks)),
-            dma((n_seq, n_chunks)),
-            dma((n_seq, n_chunks)),
-            dma((slots, n_seq, n_chunks)),
+            dma((slots, n_seq)),
+            dma((slots, n_seq)),
+            dma((n_seq,)),
+            dma((slots, n_seq, n_chunks, HALVES)),
+            dma((n_seq,)),
             dma((n_layer - 1,)),
             dma((n_layer - 1,)),
         ],

time: 38.5 us -> 34.1 us (0.89)
  Pallas kernels: 36.8 us -> 32.5 us
    pallas_call x1, Pallas kernels: 36.8 us -> 32.5 us  [on_device(): pl.pallas_call(functools.partial(kernel, sizes), out_shape=jax.ShapeDtype...]
where the time goes in v4:
time: 34.1 us; the launch traced here: 34 us
  Pallas kernels  32.5 us (95%)
  local copies, waits for them, and re-layouts  1.47 us (4%)
    pallas_call x1, Pallas kernels, on_device(): pl.pallas_call(functools.partial(kernel, sizes), out_shape=jax.ShapeDtype...  32.5 us
    unnamed x1, local copies, waits for them, and re-layouts  1.47 us

profile of v4, /device:TPU:0, one launch (start us, length us, event | category | flops | bytes accessed | tf_op | source)
XLA Modules:
  0.0 34.0 jit_solution(15720745414205195478)
XLA Ops:
  0.0 32.5 %gather_score.1 = f32[64,256]{1,0:T(8,128)} custom-call(s32[8]{0:T(128)} %owner_at.1, bf16[256,4096]{1,0:T(8,128)(2,1)} %store.1, f32[64,4096]{1,0:T(8,128)} %queries.1, f32[8,32,32]{2,1,0:T(8,128)} %eig_in_at.1, f32[8,64,64]{2,1,0:T(8,128)} %eig_out_at.1, f32[8,32,64]{2,1,0:T(8,128)} %eig_val_at.1, s32[256]{0:T(256)} %order_at.1), custom_call_target="tpu_custom_call" | custom-call | tf_op jit(solution)/shard_map/gather_score/pallas_call | solution.py:365
  32.5 1.5 %copy.9 = f32[64,256]{1,0:T(8,128)} copy(f32[64,256]{1,0:T(8,128)} %gather_score.1) | data formatting | bytes 131072

commit v5 on v4

--- a/solution.py
+++ b/solution.py
@@ -76,13 +76,14 @@
     ]
     for table in tables:
         table.start()
-    for n in range(2 * n_chunks):
-        fetch(n).start()
+    fetch(0).start()
     fetch_store = pltpu.make_async_copy(store, held, held_sem)
-    fetch_store.start()
 
     for table in tables:
         table.wait()
+    for n in range(1, 2 * n_chunks):
+        fetch(n).start()
+    fetch_store.start()
 
     def setup(slot):
         model = owner[layer * 2 + slot]
@@ -222,8 +223,13 @@
         jnp.where(here > 0, 1, 0) + jnp.where(here < n_seq - 1, 1, 0) + n_layer
     )
 
-    which = lax.broadcasted_iota(jnp.int32, perm.shape, 0)
-    perm[...] = (which == order[...].reshape(1, perm.shape[1])).astype(jnp.bfloat16)
+    def score(slot):
+        return lax.dot_general(
+            held[:, pl.ds(pl.multiple_of(slot * WIDTH, WIDTH), WIDTH)], ready[slot],
+            (((1,), (1,)), ((), ())), preferred_element_type=jnp.float32,
+        )
+
+    n_passes = (n_seq - 1) * (n_chunks + 1)
 
     def job(n, _):
         slot = jnp.where(n < n_chunks, mine, other)
@@ -247,7 +253,12 @@
                 go_up(other, here, piece, arrival)
                 go_down(other, here, piece, arrival)
 
-        @pl.when((n >= n_chunks) & (n < n_chunks + (n_seq - 1) * (n_chunks + 1)))
+        @pl.when(n == n_chunks + n_passes - 1)
+        def _():
+            fetch_store.wait()
+            total[...] = score(mine)
+
+        @pl.when((n >= n_chunks) & (n < n_chunks + n_passes))
         def _():
             pass_all(n - n_chunks)
 
@@ -262,17 +273,8 @@
 
         return 0
 
-    n_steps = n_chunks + max((n_seq - 1) * (n_chunks + 1), SPREAD * n_chunks)
+    n_steps = n_chunks + max(n_passes, SPREAD * n_chunks)
     lax.fori_loop(0, n_steps, job, 0)
-
-    def score(slot):
-        return lax.dot_general(
-            held[:, pl.ds(pl.multiple_of(slot * WIDTH, WIDTH), WIDTH)], ready[slot],
-            (((1,), (1,)), ((), ())), preferred_element_type=jnp.float32,
-        )
-
-    fetch_store.wait()
-    total[...] = score(mine)
 
     def slab(slot, source, size):
         return ready.at[slot, pl.ds(pl.multiple_of(source * rows, CHUNK), size), :]
@@ -314,6 +316,9 @@
 
     for step in range(1, n_layer):
         part(step).start()
+
+    which = lax.broadcasted_iota(jnp.int32, perm.shape, 0)
+    perm[...] = (which == order[...].reshape(1, perm.shape[1])).astype(jnp.bfloat16)
 
     each_source(lambda source, size: side_slab(mine, source, size).wait_send())
 
@@ -341,9 +346,8 @@
         part(step).wait_recv()
         result = result + sums[step - 1].astype(jnp.float32)
     high, low = split(result)
-    lowest = (result - high.astype(jnp.float32) - low.astype(jnp.float32)).astype(jnp.bfloat16)
     out[...] = sum(
-        jnp.dot(piece, perm[...], preferred_element_type=jnp.float32) for piece in (lowest, low, high)
+        jnp.dot(piece, perm[...], preferred_element_type=jnp.float32) for piece in (low, high)
     )
     for step in range(1, n_layer):
         part(step).wait_send()

time: 34.1 us -> 33.5 us (0.982)
  Pallas kernels: 32.5 us -> 31.8 us
    pallas_call x1, Pallas kernels: 32.5 us -> 31.8 us  [on_device(): pl.pallas_call(functools.partial(kernel, sizes), out_shape=jax.ShapeDtype...]
where the time goes in v5:
time: 33.5 us; the launch traced here: 33.3 us
  Pallas kernels  31.8 us (95%)
  local copies, waits for them, and re-layouts  1.47 us (4%)
    pallas_call x1, Pallas kernels, on_device(): pl.pallas_call(functools.partial(kernel, sizes), out_shape=jax.ShapeDtype...  31.8 us
    unnamed x1, local copies, waits for them, and re-layouts  1.47 us

profile of v5, /device:TPU:0, one launch (start us, length us, event | category | flops | bytes accessed | tf_op | source)
XLA Modules:
  0.0 33.3 jit_solution(15790663826316869974)
XLA Ops:
  0.0 31.8 %gather_score.1 = f32[64,256]{1,0:T(8,128)} custom-call(s32[8]{0:T(128)} %owner_at.1, bf16[256,4096]{1,0:T(8,128)(2,1)} %store.1, f32[64,4096]{1,0:T(8,128)} %queries.1, f32[8,32,32]{2,1,0:T(8,128)} %eig_in_at.1, f32[8,64,64]{2,1,0:T(8,128)} %eig_out_at.1, f32[8,32,64]{2,1,0:T(8,128)} %eig_val_at.1, s32[256]{0:T(256)} %order_at.1), custom_call_target="tpu_custom_call" | custom-call | tf_op jit(solution)/shard_map/gather_score/pallas_call | solution.py:369
  31.9 1.5 %copy.9 = f32[64,256]{1,0:T(8,128)} copy(f32[64,256]{1,0:T(8,128)} %gather_score.1) | data formatting | bytes 131072

commit v6 on v5

--- a/solution.py
+++ b/solution.py
@@ -14,7 +14,7 @@
 PAIRS = A // 2
 CHUNK = 16
 GROUP = 16
-HALVES = 1
+HALVES = 2
 SPREAD = 2
 MESH = pl.DeviceIdType.MESH
 EXACT = lax.Precision.HIGHEST
@@ -207,10 +207,13 @@
     def pass_all(n):
         distance, k = 1 + n // (n_chunks + 1), lax.rem(n, n_chunks + 1)
         below, above = here - distance, here + distance
-        for source, exists, is_end, way in (
-            (below, below >= 0, below == 0, go_up),
-            (above, above < n_seq, above == n_seq - 1, go_down),
+        low = here < n_seq // 2
+        for source, exists, is_end, way, when in (
+            (above, above < n_seq, above == n_seq - 1, go_down, low),
+            (below, below >= 0, below == 0, go_up, True),
+            (above, above < n_seq, above == n_seq - 1, go_down, jnp.logical_not(low)),
         ):
+            exists = exists & when
             @pl.when(exists & (k < n_chunks))
             def _():
                 pass_on(mine, source, k, is_end, (way,))
@@ -314,7 +317,7 @@
             recv_sem=part_arrive.at[step - 1], device_id={"layer": to}, device_id_type=MESH,
         )
 
-    for step in range(1, n_layer):
+    for step in (*range(2, n_layer), 1):
         part(step).start()
 
     which = lax.broadcasted_iota(jnp.int32, perm.shape, 0)

time: 33.5 us -> 33.5 us (level)
  no operation moved by 1% of the time
where the time goes in v6:
time: 33.5 us; the launch traced here: 33.4 us
  Pallas kernels  31.9 us (95%)
  local copies, waits for them, and re-layouts  1.47 us (4%)
    pallas_call x1, Pallas kernels, on_device(): pl.pallas_call(functools.partial(kernel, sizes), out_shape=jax.ShapeDtype...  31.9 us
    unnamed x1, local copies, waits for them, and re-layouts  1.47 us

profile of v6, /device:TPU:0, one launch (start us, length us, event | category | flops | bytes accessed | tf_op | source)
XLA Modules:
  0.0 33.4 jit_solution(10071606659378653859)
XLA Ops:
  0.0 31.9 %gather_score.1 = f32[64,256]{1,0:T(8,128)} custom-call(s32[8]{0:T(128)} %owner_at.1, bf16[256,4096]{1,0:T(8,128)(2,1)} %store.1, f32[64,4096]{1,0:T(8,128)} %queries.1, f32[8,32,32]{2,1,0:T(8,128)} %eig_in_at.1, f32[8,64,64]{2,1,0:T(8,128)} %eig_out_at.1, f32[8,32,64]{2,1,0:T(8,128)} %eig_val_at.1, s32[256]{0:T(256)} %order_at.1), custom_call_target="tpu_custom_call" | custom-call | tf_op jit(solution)/shard_map/gather_score/pallas_call | solution.py:372
  31.9 1.5 %copy.9 = f32[64,256]{1,0:T(8,128)} copy(f32[64,256]{1,0:T(8,128)} %gather_score.1) | data formatting | bytes 131072
